TPU v7x, 32 devices: a whole 2x2x4 slice. The times are simulated.
32 devices in a mesh: groups: 2 (over x), enc: 16 (over z, y, core).
Axes of the slice: x: 2, y: 2, z: 4, core: 2. Of those that a mesh axis runs over, the one named last changes fastest.
Arguments:
- cache_rows: bfloat16 [4096, 2, 1280], P(('groups', 'enc')), parts along dimension 0, may hold values from -6 to 6
- hit_owner: int32 [8192, 1], P(('groups', 'enc')), parts along dimension 0, may hold values from 0 to 15; in each aligned block of 256 rows (0 to 255, 256 to 511, ...) at most 32 rows name the same one
- hit_slot: int32 [8192], P(('groups', 'enc')), parts along dimension 0, may hold values from 0 to 127
- miss_pixels: bfloat16 [4096, 2, 588], P(('groups', 'enc')), parts along dimension 0, may hold values from -6 to 6
- miss_encoder: int32 [4096, 1], P(('groups', 'enc')), parts along dimension 0, may hold values from 0 to 15; in each aligned block of 128 rows (0 to 127, 128 to 255, ...) at most 16 rows name the same one
- patch_weight: bfloat16 [588, 1280], replicated, may hold values from -0.25 to 0.25
- position: float32 [2, 1280], replicated, may hold values from -6 to 6
- norm_gain: float32 [1280], replicated, may hold values from 0.1 to 1.9
- norm_bias: float32 [1280], replicated, may hold values from -3 to 3
- pair_weight: bfloat16 [1280, 2048], replicated, may hold values from -0.15625 to 0.15625
Outputs:
- hit_pairs: bfloat16 [8192, 2, 2048], P(('groups', 'enc')), parts along dimension 0
- miss_pairs: bfloat16 [4096, 2, 2048], P(('groups', 'enc')), parts along dimension 0
- fresh_cache: bfloat16 [8192, 2, 1280], P(('groups', 'enc')), parts along dimension 0
There are 2 independent parts, one for each index of `groups`. A program takes and returns all parts, laid end to end along the dimension named above; an argument that names none is the same for every part. Nothing has to cross between parts.
Inputs may be any that keep to these rules, and one draw needn't show every extreme that they name: `hit_owner`: in the rows of one device no cache shard is named more than 32 times, and some device names one exactly 32 times. `miss_encoder`: in the rows of one device no encoder shard is named more than 16 times, and some device names one exactly 16 times.
All inputs are finite; a program needn't handle non-finite values.
Results may differ from a plain program's by a relative error of at most 0.0051.
Values may be sent and summed in bfloat16 or wider, within the bound.
A program may use at most 64 MiB of HBM per device.

v0:
```python
import jax
import jax.numpy as jnp
from jax import lax
from jax.sharding import PartitionSpec as P


def layer_norm(values, gain_row, bias_row):
    average = jnp.mean(values, axis=-1, keepdims=True)
    centered = values - average
    variance = jnp.mean(centered * centered, axis=-1, keepdims=True)
    return centered / jnp.sqrt(variance + 1e-05) * gain_row + bias_row


def encode_patches(pixel_rows, patch_weight, position, norm_gain, norm_bias):
    leading = pixel_rows.shape[:-1]
    flat_rows = pixel_rows.reshape(-1, pixel_rows.shape[-1])
    embedded = jnp.dot(flat_rows, patch_weight, preferred_element_type=jnp.float32)
    embedded = embedded.reshape(leading + (patch_weight.shape[1],)) + position
    return layer_norm(embedded, norm_gain, norm_bias).astype(jnp.bfloat16)


def project_pairs(embed_rows, pair_weight):
    leading = embed_rows.shape[:-1]
    flat_rows = embed_rows.reshape(-1, embed_rows.shape[-1])
    projected = jnp.dot(flat_rows, pair_weight, preferred_element_type=jnp.float32)
    return projected.astype(jnp.bfloat16).reshape(leading + (pair_weight.shape[1],))


def buffer_places(targets, capacity):
    item_count = targets.shape[0]
    matches = targets[:, None] == targets[None, :]
    column_ids = lax.broadcasted_iota(jnp.int32, (item_count, item_count), 1)
    row_ids = lax.broadcasted_iota(jnp.int32, (item_count, item_count), 0)
    ranking = jnp.sum(jnp.where(matches & (column_ids < row_ids), 1, 0), axis=1).astype(jnp.int32)
    return targets * capacity + ranking


def buffer_sources(places, buffer_width):
    item_count = places.shape[0]
    slot_table = places[:, None] == lax.broadcasted_iota(jnp.int32, (item_count, buffer_width), 1)
    item_ids = lax.broadcasted_iota(jnp.int32, (item_count, buffer_width), 0)
    anchor = jnp.sum(jnp.where(slot_table, item_ids, 0), axis=0)
    occupied = jnp.any(slot_table, axis=0)
    return (anchor, occupied)


def fill_buffer(item_rows, anchor, occupied):
    gathered_items = jnp.take(item_rows, anchor, axis=0)
    slot_mask = occupied.reshape((-1,) + (1,) * (item_rows.ndim - 1))
    return jnp.where(slot_mask, gathered_items, jnp.zeros_like(gathered_items))


def local(
    cache_rows,
    hit_owner,
    hit_slot,
    miss_pixels,
    miss_encoder,
    patch_weight,
    position,
    norm_gain,
    norm_bias,
    pair_weight,
):
    peer_count = lax.axis_size("enc")
    hit_count = hit_slot.shape[0]
    miss_count = miss_encoder.shape[0]
    hit_cap = max(2, 2 * hit_count // peer_count)
    miss_cap = max(2, 2 * miss_count // peer_count)
    hit_places = buffer_places(hit_owner[:, 0], hit_cap)
    hit_anchor, hit_occupied = buffer_sources(hit_places, peer_count * hit_cap)
    wanted = jnp.where(hit_occupied, jnp.take(hit_slot, hit_anchor) + 1, 0)
    asked_slots = lax.all_to_all(
        wanted.reshape(peer_count, hit_cap), "enc", split_axis=0, concat_axis=0, tiled=True
    )
    asked_flat = asked_slots.reshape(-1)
    stored = jnp.take(cache_rows, jnp.maximum(asked_flat - 1, 0), axis=0)
    stored = jnp.where((asked_flat > 0).reshape(-1, 1, 1), stored, jnp.zeros_like(stored))
    stored = stored.reshape((peer_count, hit_cap) + cache_rows.shape[1:])
    answered = lax.all_to_all(
        project_pairs(stored, pair_weight), "enc", split_axis=0, concat_axis=0, tiled=True
    )
    answered = answered.reshape((peer_count * hit_cap,) + answered.shape[2:])
    hit_pairs = jnp.take(answered, hit_places, axis=0)
    miss_places = buffer_places(miss_encoder[:, 0], miss_cap)
    miss_anchor, miss_occupied = buffer_sources(miss_places, peer_count * miss_cap)
    outgoing = fill_buffer(miss_pixels, miss_anchor, miss_occupied)
    outgoing = outgoing.reshape((peer_count, miss_cap) + miss_pixels.shape[1:])
    live_flags = miss_occupied.astype(jnp.bfloat16).reshape(peer_count, miss_cap)
    pixel_block = lax.all_to_all(outgoing, "enc", split_axis=0, concat_axis=0, tiled=True)
    flag_block = lax.all_to_all(live_flags, "enc", split_axis=0, concat_axis=0, tiled=True)
    encoded_block = encode_patches(pixel_block, patch_weight, position, norm_gain, norm_bias)
    keep_mask = flag_block[:, :, None, None] > 0
    fresh_block = jnp.where(keep_mask, encoded_block, jnp.zeros_like(encoded_block))
    returned = lax.all_to_all(fresh_block, "enc", split_axis=0, concat_axis=0, tiled=True)
    returned = returned.reshape((peer_count * miss_cap,) + returned.shape[2:])
    miss_pairs = project_pairs(jnp.take(returned, miss_places, axis=0), pair_weight)
    fresh_cache = fresh_block.reshape((peer_count * miss_cap,) + fresh_block.shape[2:])
    return (hit_pairs, miss_pairs, fresh_cache)


def solution(mesh):
    placed = (
        P(("groups", "enc"), None, None),
        P(("groups", "enc"), None),
        P(("groups", "enc")),
        P(("groups", "enc"), None, None),
        P(("groups", "enc"), None),
        P(),
        P(),
        P(),
        P(),
        P(),
    )
    return jax.shard_map(
        local,
        mesh=mesh,
        in_specs=placed,
        out_specs=(
            P(("groups", "enc"), None, None),
            P(("groups", "enc"), None, None),
            P(("groups", "enc"), None, None),
        ),
        check_vma=False,
    )
```

profile of v0, /device:TPU:15, one launch (start us, length us, event | category | flops | bytes accessed | tf_op | source)
XLA Modules:
  0.0 212.1 jit_solution(1018309247597548680)
XLA Ops:
  3.1 6.6 %all-to-all-start.2 = ((bf16[16,1,16]{2,1,0:T(2,128)(2,1)}), bf16[16,1,16]{2,1,0:T(2,128)(2,1)S(1)}, u32[]{:S(2)}, u32[]{:S(2)}) async-start(bf16[16,1,16]{2,1,0:T(2,128)(2,1)} %reshape.285), calls=%async_computation.2 | async-start | bytes 16384 | tf_op jit(solution)/shard_map/all_to_all | solution.py:91
  9.8 1.5 copy.53
  11.5 2.1 gather_fusion.3
  14.8 6.0 %all-to-all-start.3 = ((bf16[16,16,2,588]{3,1,2,0:T(8,128)(2,1)}), bf16[16,16,2,588]{3,1,2,0:T(8,128)(2,1)S(1)}, u32[]{:S(2)}, u32[]{:S(2)}) async-start(bf16[16,16,2,588]{3,1,2,0:T(8,128)(2,1)} %fusion.8), calls=%async_computation.3 | async-start | bytes 1310720 | tf_op jit(solution)/shard_map/all_to_all | solution.py:90
  21.3 3.5 %gather_fusion = s32[512]{0:T(512)S(1)} fusion(s32[256]{0:T(256)S(1)} %copy-done.1, s32[1024]{0:T(1024)S(1)} %pad_clamp_fusion.4), kind=kCustom, calls=%fused_computation | custom fusion | bytes 6144 | tf_op jit(solution)/shard_map/jit(_take)/gather | solution.py:72
  25.5 11.7 %all-to-all-done.3 = bf16[16,16,2,588]{3,1,2,0:T(8,128)(2,1)S(1)} async-done(((bf16[16,16,2,588]{3,1,2,0:T(8,128)(2,1)}), bf16[16,16,2,588]{3,1,2,0:T(8,128)(2,1)S(1)}, u32[]{:S(2)}, u32[]{:S(2)}) %all-to-all-start.3) | async-done | bytes 602144 | tf_op jit(solution)/shard_map/all_to_all | solution.py:90
  37.2 5.0 %all-to-all-start = ((s32[16,1,32]{2,1,0:T(1,128)}), s32[16,1,32]{2,1,0:T(1,128)S(1)}, u32[]{:S(2)}, u32[]{:S(2)}) async-start(s32[16,1,32]{2,1,0:T(1,128)} %bitcast.5), calls=%async_computation | async-start | bytes 16384 | tf_op jit(solution)/shard_map/all_to_all | solution.py:73
  42.2 1.3 fusion.21
  44.3 1.6 fusion.7
  45.9 6.2 %all-to-all-start.4 = ((bf16[16,16,2,1280]{3,1,2,0:T(8,128)(2,1)}), bf16[16,16,2,1280]{3,1,2,0:T(8,128)(2,1)S(1)}, u32[]{:S(2)}, u32[]{:S(2)}) async-start(bf16[16,16,2,1280]{3,1,2,0:T(8,128)(2,1)} %fusion.7), calls=%async_computation.4 | async-start | bytes 2621440 | tf_op jit(solution)/shard_map/all_to_all | solution.py:95
  52.3 17.6 %gather_fusion.1 = bf16[512,2,1280]{2,1,0:T(2,128)(2,1)} fusion(bf16[128,2,1280]{2,1,0:T(2,128)(2,1)S(1)} %copy-done.2, s32[1024]{0:T(1024)S(1)} %pad_clamp_fusion.3), kind=kCustom, calls=%fused_computation.1 | custom fusion | bytes 5244928 | tf_op jit(solution)/shard_map/jit(_take)/gather | solution.py:77
  69.9 6.7 %gather.31 = bf16[1024,1280]{1,0:T(8,128)(2,1)} reshape(bf16[512,2,1280]{2,1,0:T(2,128)(2,1)} %gather_fusion.1) | data formatting | bytes 5242880 | tf_op jit(solution)/shard_map/jit(_take)/gather | solution.py:77
  77.4 10.4 %convolution_convert_fusion = bf16[1024,2048]{1,0:T(8,128)(2,1)} fusion(bf16[1280,2048]{1,0:T(8,128)(2,1)} %param.19, bf16[1024,1280]{1,0:T(8,128)(2,1)} %gather.31, pred[1024]{0:T(1024)(128)(4,1)S(1)} %broadcast_in_dim.136, pred[1024]{0:T(1024)(128)(4,1)S(1)} %broadcast_in_dim.133), kind=kOutput, calls=%fused_computation.6 | convolution fusion | flops 5373427712 | bytes 12060672 | tf_op jit(solution)/shard_map/dot_general | solution.py:25
  87.7 7.6 %reshape.237 = bf16[16,32,2,2048]{3,2,1,0:T(2,128)(2,1)} reshape(bf16[1024,2048]{1,0:T(8,128)(2,1)} %convolution_convert_fusion) | data formatting | bytes 8388608 | tf_op jit(solution)/shard_map/reshape | solution.py:26
  95.4 6.6 %all-to-all-start.1 = ((bf16[16,32,2,2048]{3,2,1,0:T(2,128)(2,1)}), bf16[16,32,2,2048]{3,2,1,0:T(2,128)(2,1)}, u32[]{:S(2)}, u32[]{:S(2)}) async-start(bf16[16,32,2,2048]{3,2,1,0:T(2,128)(2,1)} %reshape.237), calls=%async_computation.1 | async-start | bytes 8388608 | tf_op jit(solution)/shard_map/all_to_all | solution.py:80
  102.3 1.4 copy.58
  103.7 2.4 %copy.59 = bf16[256,2,1280]{2,1,0:T(2,128)(2,1)} copy(bf16[256,2,1280]{2,0,1:T(8,128)(2,1)S(1)} %bitcast.48) | data formatting | bytes 2621440
  106.2 1.3 copy.57
  107.6 2.0 gather_fusion.4
  110.6 4.3 %convolution_convert_fusion.1 = bf16[256,2048]{1,0:T(8,128)(2,1)S(1)} fusion(bf16[1280,2048]{1,0:T(8,128)(2,1)} %param.19, bf16[256,1280]{1,0:T(8,128)(2,1)} %gather.36, pred[256]{0:T(512)(128)(4,1)S(1)} %broadcast_in_dim.144), kind=kOutput, calls=%fused_computation.14 | convolution fusion | flops 1343029248 | bytes 6947072 | tf_op jit(solution)/shard_map/dot_general | solution.py:25
  114.9 1.5 reshape.240
  116.4 78.1 %all-to-all-done.1 = bf16[16,32,2,2048]{3,2,1,0:T(2,128)(2,1)} async-done(((bf16[16,32,2,2048]{3,2,1,0:T(2,128)(2,1)}), bf16[16,32,2,2048]{3,2,1,0:T(2,128)(2,1)}, u32[]{:S(2)}, u32[]{:S(2)}) %all-to-all-start.1) | async-done | bytes 4194336 | tf_op jit(solution)/shard_map/all_to_all | solution.py:80
  194.5 12.7 %gather_fusion.2 = bf16[256,2,2048]{2,1,0:T(2,128)(2,1)} fusion(bf16[512,2,2048]{2,1,0:T(2,128)(2,1)} %bitcast.8, s32[1024]{0:T(1024)S(1)} %pad_clamp_fusion.2), kind=kCustom, calls=%fused_computation.2 | custom fusion | bytes 4195328 | tf_op jit(solution)/shard_map/jit(_take)/gather | solution.py:84
  207.1 4.9 %broadcast_select_fusion = bf16[256,2,2048]{2,1,0:T(2,128)(2,1)} fusion(bf16[256,2,2048]{2,1,0:T(2,128)(2,1)} %gather_fusion.2, pred[256]{0:T(512)(128)(4,1)S(1)} %get-tuple-element.18), kind=kLoop, calls=%fused_computation.5 | loop fusion | flops 1048576 | bytes 4194560 | tf_op jit(solution)/shard_map/jit(_take)/select_n | solution.py:84
  (62 shorter events, 8.2 us)
Async XLA Ops:
  0.6 41.6 %copy-start = (bf16[588,1280]{1,0:T(8,128)(2,1)S(1)}, bf16[588,1280]{1,0:T(8,128)(2,1)}, u32[]{:S(2)}) copy-start(bf16[588,1280]{1,0:T(8,128)(2,1)} %param.15) | copy-start | bytes 4515844
  0.6 13.9 %copy-start.3 = (s32[256,1]{0,1:T(1,128)S(1)}, s32[256,1]{0,1:T(1,128)}, u32[]{:S(2)}) copy-start(s32[256,1]{0,1:T(1,128)} %param.11) | copy-start | bytes 3076
  0.7 20.7 %copy-start.1 = (s32[256]{0:T(256)S(1)}, s32[256]{0:T(256)}, u32[]{:S(2)}) copy-start(s32[256]{0:T(256)} %param.12) | copy-start | bytes 3076
  3.1 11.7 %all-to-all-start.2 = ((bf16[16,1,16]{2,1,0:T(2,128)(2,1)}), bf16[16,1,16]{2,1,0:T(2,128)(2,1)S(1)}, u32[]{:S(2)}, u32[]{:S(2)}) async-start(bf16[16,1,16]{2,1,0:T(2,128)(2,1)} %reshape.285), calls=%async_computation.2 | async-start | bytes 16384 | tf_op jit(solution)/shard_map/all_to_all | solution.py:91
  13.5 28.7 %copy-start.7 = (f32[2,1280]{1,0:T(2,128)S(1)}, f32[2,1280]{1,0:T(2,128)}, u32[]{:S(2)}) copy-start(f32[2,1280]{1,0:T(2,128)} %param.16) | copy-start | bytes 30724
  14.8 22.5 %all-to-all-start.3 = ((bf16[16,16,2,588]{3,1,2,0:T(8,128)(2,1)}), bf16[16,16,2,588]{3,1,2,0:T(8,128)(2,1)S(1)}, u32[]{:S(2)}, u32[]{:S(2)}) async-start(bf16[16,16,2,588]{3,1,2,0:T(8,128)(2,1)} %fusion.8), calls=%async_computation.3 | async-start | bytes 1310720 | tf_op jit(solution)/shard_map/all_to_all | solution.py:90
  37.2 8.7 %all-to-all-start = ((s32[16,1,32]{2,1,0:T(1,128)}), s32[16,1,32]{2,1,0:T(1,128)S(1)}, u32[]{:S(2)}, u32[]{:S(2)}) async-start(s32[16,1,32]{2,1,0:T(1,128)} %bitcast.5), calls=%async_computation | async-start | bytes 16384 | tf_op jit(solution)/shard_map/all_to_all | solution.py:73
  43.5 0.7 copy-start.4
  43.5 0.7 copy-start.5
  44.3 8.0 %copy-start.2 = (bf16[128,2,1280]{2,1,0:T(2,128)(2,1)S(1)}, bf16[128,2,1280]{2,1,0:T(2,128)(2,1)}, u32[]{:S(2)}) copy-start(bf16[128,2,1280]{2,1,0:T(2,128)(2,1)} %param.10) | copy-start | bytes 1966084
  45.9 49.5 %all-to-all-start.4 = ((bf16[16,16,2,1280]{3,1,2,0:T(8,128)(2,1)}), bf16[16,16,2,1280]{3,1,2,0:T(8,128)(2,1)S(1)}, u32[]{:S(2)}, u32[]{:S(2)}) async-start(bf16[16,16,2,1280]{3,1,2,0:T(8,128)(2,1)} %fusion.7), calls=%async_computation.4 | async-start | bytes 2621440 | tf_op jit(solution)/shard_map/all_to_all | solution.py:95
  95.4 6.6 %copy-start.6 = (s32[128,1]{0,1:T(1,128)S(1)}, s32[128,1]{0,1:T(1,128)}, u32[]{:S(2)}) copy-start(s32[128,1]{0,1:T(1,128)} %param.14) | copy-start | bytes 1540
  95.4 99.1 %all-to-all-start.1 = ((bf16[16,32,2,2048]{3,2,1,0:T(2,128)(2,1)}), bf16[16,32,2,2048]{3,2,1,0:T(2,128)(2,1)}, u32[]{:S(2)}, u32[]{:S(2)}) async-start(bf16[16,32,2,2048]{3,2,1,0:T(2,128)(2,1)} %reshape.237), calls=%async_computation.1 | async-start | bytes 8388608 | tf_op jit(solution)/shard_map/all_to_all | solution.py:80
where the time goes:
time: 213 us; the launch traced here: 212 us
  waiting for transfers between devices  89.9 us (42%)
  local copies, waits for them, and re-layouts  63.9 us (30%)
  starting transfers between devices  30.4 us (14%)
  matrix products  15.9 us (7%)
  other arithmetic  11.1 us (5%)
    all_to_all x1, waiting for transfers between devices, local(): lax.all_to_all(project_pairs(stored, pair_weight), 'enc', split_axis=0, c...  78.1 us
    gather x2, local copies, waits for them, and re-layouts, local(): stored = jnp.take(cache_rows, jnp.maximum(asked_flat - 1, 0), axis=0)  24.3 us
    dot_general x2, matrix products, project_pairs(): jnp.dot(flat_rows, pair_weight, preferred_element_type=jnp.float32)  14.6 us
    gather x1, local copies, waits for them, and re-layouts, local(): hit_pairs = jnp.take(answered, hit_places, axis=0)  12.7 us
    all_to_all x1, waiting for transfers between devices, local(): lax.all_to_all(outgoing, 'enc', split_axis=0, concat_axis=0, tiled=True)  11.7 us
    reshape x2, local copies, waits for them, and re-layouts, project_pairs(): projected.astype(jnp.bfloat16).reshape(leading + (pair_weight.shape[1],))  9.13 us
    all_to_all x1, starting transfers between devices, local(): lax.all_to_all(project_pairs(stored, pair_weight), 'enc', split_axis=0, c...  6.64 us
    all_to_all x1, starting transfers between devices, local(): lax.all_to_all(live_flags, 'enc', split_axis=0, concat_axis=0, tiled=True)  6.55 us
  transfers between devices with their start and end apart: 5, of which 2 were waited for; matrix products, arithmetic and copies ran while one was open for 33% of the time, Pallas kernels for 0%

commit v1 on v0

v1 whole, which is shorter than its diff:
```python
import jax
import jax.numpy as jnp
from jax import lax
from jax.sharding import PartitionSpec as P


def layer_norm(values, gain_row, bias_row):
    average = jnp.mean(values, axis=-1, keepdims=True)
    centered = values - average
    variance = jnp.mean(centered * centered, axis=-1, keepdims=True)
    return centered / jnp.sqrt(variance + 1e-05) * gain_row + bias_row


def encode_patches(pixel_rows, patch_weight, position, norm_gain, norm_bias):
    leading = pixel_rows.shape[:-1]
    flat_rows = pixel_rows.reshape(-1, pixel_rows.shape[-1])
    embedded = jnp.dot(flat_rows, patch_weight, preferred_element_type=jnp.float32)
    embedded = embedded.reshape(leading + (patch_weight.shape[1],)) + position
    return layer_norm(embedded, norm_gain, norm_bias).astype(jnp.bfloat16)


def project_pairs(embed_rows, pair_weight):
    leading = embed_rows.shape[:-1]
    flat_rows = embed_rows.reshape(-1, embed_rows.shape[-1])
    projected = jnp.dot(flat_rows, pair_weight, preferred_element_type=jnp.float32)
    return projected.astype(jnp.bfloat16).reshape(leading + (pair_weight.shape[1],))


def fill_places(targets, capacity):
    count = targets.shape[0]
    item = lax.broadcasted_iota(jnp.int32, (count, count), 1)
    row = lax.broadcasted_iota(jnp.int32, (count, count), 0)
    matches = targets[:, None] == targets[None, :]
    rank = jnp.sum(jnp.where(matches & (item < row), 1, 0), axis=1).astype(jnp.int32)
    return targets * capacity + rank


def slots_of(places, width):
    count = places.shape[0]
    return places[None, :] == lax.broadcasted_iota(jnp.int32, (width, count), 0)


def hits_by_gather(cache_rows, hit_owner, hit_slot, pair_weight):
    gathered = lax.all_gather(cache_rows, "enc", axis=0, tiled=True)
    rows = jnp.take(gathered, hit_owner * cache_rows.shape[0] + hit_slot, axis=0)
    return project_pairs(rows, pair_weight)


def hits_by_request(cache_rows, hit_owner, hit_slot, pair_weight):
    peers = lax.axis_size("enc")
    cap = max(2, 2 * hit_slot.shape[0] // peers)
    places = fill_places(hit_owner, cap)
    table = slots_of(places, peers * cap)
    wanted = jnp.sum(jnp.where(table, hit_slot[None, :], 0), axis=1).reshape(peers, cap)
    asked = lax.all_to_all(wanted, "enc", split_axis=0, concat_axis=0, tiled=True)
    stored = jnp.take(cache_rows, asked.reshape(-1), axis=0)
    stored = stored.reshape((peers, cap) + cache_rows.shape[1:])
    answered = lax.all_to_all(stored, "enc", split_axis=0, concat_axis=0, tiled=True)
    answered = answered.reshape((peers * cap,) + answered.shape[2:])
    return project_pairs(jnp.take(answered, places, axis=0), pair_weight)


def local(
    cache_rows,
    hit_owner,
    hit_slot,
    miss_pixels,
    miss_encoder,
    patch_weight,
    position,
    norm_gain,
    norm_bias,
    pair_weight,
):
    peers = lax.axis_size("enc")
    count, patches, pixels = miss_pixels.shape
    cap = max(2, 2 * count // peers)
    width = peers * cap
    table = slots_of(fill_places(miss_encoder[:, 0], cap), width).astype(jnp.bfloat16)
    items = jnp.concatenate(
        [miss_pixels.reshape(count, patches * pixels), jnp.ones((count, 1), jnp.bfloat16)], axis=1
    )
    outgoing = jnp.dot(table, items, preferred_element_type=jnp.float32).astype(jnp.bfloat16)
    outgoing = outgoing.reshape(peers, cap, items.shape[1])
    incoming = lax.all_to_all(outgoing, "enc", split_axis=0, concat_axis=0, tiled=True)
    incoming = incoming.reshape(width, items.shape[1])
    encode = lambda rows: encode_patches(rows, patch_weight, position, norm_gain, norm_bias)
    hits = hits_by_gather if peers <= 16 else hits_by_request
    hit_pairs = hits(cache_rows, hit_owner[:, 0], hit_slot, pair_weight)
    miss_pairs = project_pairs(encode(miss_pixels), pair_weight)
    fresh = encode(incoming[:, : patches * pixels].reshape(width, patches, pixels))
    live = incoming[:, patches * pixels :].reshape(width, 1, 1) > 0
    fresh_cache = jnp.where(live, fresh, jnp.zeros_like(fresh))
    return (hit_pairs, miss_pairs, fresh_cache)


def solution(mesh):
    placed = (
        P(("groups", "enc"), None, None),
        P(("groups", "enc"), None),
        P(("groups", "enc")),
        P(("groups", "enc"), None, None),
        P(("groups", "enc"), None),
        P(),
        P(),
        P(),
        P(),
        P(),
    )
    return jax.shard_map(
        local,
        mesh=mesh,
        in_specs=placed,
        out_specs=(
            P(("groups", "enc"), None, None),
            P(("groups", "enc"), None, None),
            P(("groups", "enc"), None, None),
        ),
        check_vma=False,
    )
```

time: 213 us -> 139 us (0.65)
  the two profiles are of different devices: /device:TPU:15 before, /device:TPU:0 now
where the time goes in v1:
time: 139 us
  waiting for transfers between devices  76.7 us (55%)
  local copies, waits for them, and re-layouts  22.5 us (16%)
  matrix products  14.8 us (11%)
  between operations  14.3 us (10%)
  starting transfers between devices  7.42 us (5%)
  other arithmetic  3.34 us (2%)
    all_gather x1, waiting for transfers between devices, hits_by_gather(): gathered = lax.all_gather(cache_rows, 'enc', axis=0, tiled=True)  62.5 us
    all_to_all x1, waiting for transfers between devices, local(): lax.all_to_all(outgoing, 'enc', split_axis=0, concat_axis=0, tiled=True)  13.5 us
    dot_general x2, matrix products, project_pairs(): jnp.dot(flat_rows, pair_weight, preferred_element_type=jnp.float32)  11.4 us
    gather x2, local copies, waits for them, and re-layouts, hits_by_gather(): jnp.take(gathered, hit_owner * cache_rows.shape[0] + hit_slot, axis=0)  8.76 us
    all_to_all x1, starting transfers between devices, local(): lax.all_to_all(outgoing, 'enc', split_axis=0, concat_axis=0, tiled=True)  7.38 us
    reshape x2, local copies, waits for them, and re-layouts, project_pairs(): projected.astype(jnp.bfloat16).reshape(leading + (pair_weight.shape[1],))  5.88 us
    unnamed x18, local copies, waits for them, and re-layouts  3.46 us
    dot_general x2, matrix products, encode_patches(): jnp.dot(flat_rows, patch_weight, preferred_element_type=jnp.float32)  3.08 us
  transfers between devices with their start and end apart: 2, of which 2 were waited for; matrix products, arithmetic and copies ran while one was open for 15% of the time, Pallas kernels for 0%

profile of v1, /device:TPU:0, one launch (start us, length us, event | category | flops | bytes accessed | tf_op | source)
XLA Modules:
  0.0 139.0 jit_solution(493085812925876108)
XLA Ops:
  7.2 0.7 all-gather.2.cloned.1.call-update
  7.9 1.0 copy.33
  9.2 0.3 convolution_convert_fusion.1
  9.5 1.1 copy.36
  10.6 7.4 %all-to-all-start = ((bf16[16,16,1177]{2,1,0:T(8,128)(2,1)}), bf16[16,16,1177]{2,1,0:T(8,128)(2,1)S(1)}, u32[]{:S(2)}, u32[]{:S(2)}) async-start(bf16[16,16,1177]{2,1,0:T(8,128)(2,1)} %bitcast.3), calls=%async_computation | async-start | bytes 1310720 | tf_op jit(solution)/shard_map/all_to_all | solution.py:85
  18.1 1.8 %fusion.13 = (f32[128,2]{0,1:T(2,128)S(1)}, f32[128,2,1280]{2,0,1:T(8,128)S(1)}) fusion(f32[2,1280]{1,0:T(2,128)S(1)} %copy-done.3, bf16[588,1280]{1,0:T(8,128)(2,1)S(1)} %copy-done, bf16[128,2,588]{0,1,2:T(2,128)(2,1)} %param.13), kind=kOutput, calls=%fused_computation.36 | convolution fusion | flops 386006784 | bytes 3128320 | tf_op jit(solution)/shard_map/dot_general | solution.py:17
  19.9 0.3 multiply_reduce_fusion.1
  20.3 0.7 broadcast_in_dim.48
  21.0 0.3 add_convert_fusion.1
  21.3 0.7 copy.34
  22.0 1.1 reshape.88
  23.1 4.2 %convolution_convert_fusion.2 = bf16[256,2048]{1,0:T(8,128)(2,1)S(1)} fusion(bf16[256,1280]{1,0:T(8,128)(2,1)} %reshape.88, bf16[1280,2048]{1,0:T(8,128)(2,1)} %param.19), kind=kOutput, calls=%fused_computation.7 | convolution fusion | flops 1342701568 | bytes 6946816 | tf_op jit(solution)/shard_map/dot_general | solution.py:25
  27.3 1.5 %reshape.89 = bf16[128,2,2048]{2,1,0:T(2,128)(2,1)} reshape(bf16[256,2048]{1,0:T(8,128)(2,1)S(1)} %convolution_convert_fusion.2) | data formatting | bytes 2097152 | tf_op jit(solution)/shard_map/reshape | solution.py:26
  28.8 13.5 %all-to-all-done = bf16[16,16,1177]{2,1,0:T(8,128)(2,1)S(1)} async-done(((bf16[16,16,1177]{2,1,0:T(8,128)(2,1)}), bf16[16,16,1177]{2,1,0:T(8,128)(2,1)S(1)}, u32[]{:S(2)}, u32[]{:S(2)}) %all-to-all-start) | async-done | bytes 602656 | tf_op jit(solution)/shard_map/all_to_all | solution.py:85
  42.3 0.7 reshape.103
  43.2 1.3 fusion.14
  44.5 0.4 multiply_reduce_fusion
  44.9 2.0 %fusion.3 = bf16[256,2,1280]{2,0,1:T(8,128)(2,1)S(1)} fusion(f32[1280]{0:T(1024)S(1)} %copy-done.1, f32[1280]{0:T(1024)S(1)} %copy-done.2, f32[256,2]{0,1:T(2,128)S(1)} %add_sqrt_fusion, f32[256,2,1280]{2,0,1:T(8,128)S(1)} %get-tuple-element.23, f32[256,2]{0,1:T(2,128)S(1)} %broadcast_multiply_fusion, pred[256]{0:T(512)(128)(4,1)S(1)} %compare_reduce_fusion), kind=kLoop, calls=%fused_computation.13 | loop fusion | flops 3932160 | bytes 3946752 | tf_op jit(solution)/shard_map/jit(_where)/select_n | solution.py:93
  46.9 2.4 %copy.38 = bf16[256,2,1280]{2,1,0:T(2,128)(2,1)} copy(bf16[256,2,1280]{2,0,1:T(8,128)(2,1)S(1)} %fusion.3) | data formatting | bytes 2621440
  49.3 62.5 %all-gather.2.cloned.1.call-done = bf16[2048,2,1280]{2,1,0:T(2,128)(2,1)} async-done(((bf16[128,2,1280]{2,1,0:T(2,128)(2,1)}), bf16[2048,2,1280]{2,1,0:T(2,128)(2,1)}) %all-gather.2.cloned.1.call-update) | async-done | bytes 10485776 | tf_op jit(solution)/shard_map/all_gather | solution.py:44
  111.8 7.4 %gather_fusion = bf16[256,2,1280]{2,1,0:T(2,128)(2,1)S(1)} fusion(bf16[2048,2,1280]{2,1,0:T(2,128)(2,1)} %all-gather.2.cloned.1.call-done, s32[1024]{0:T(1024)S(1)} %pad_clamp_fusion), kind=kCustom, calls=%fused_computation | custom fusion | bytes 2622464 | tf_op jit(solution)/shard_map/jit(_take)/gather | solution.py:45
  119.3 1.4 gather.7
  120.6 7.2 %convolution_convert_fusion = bf16[512,2048]{1,0:T(8,128)(2,1)} fusion(bf16[1280,2048]{1,0:T(8,128)(2,1)} %param.19, bf16[512,1280]{1,0:T(8,128)(2,1)} %gather.7, pred[512]{0:T(512)(128)(4,1)S(1)} %copy-done.6), kind=kOutput, calls=%fused_computation.2 | convolution fusion | flops 2686058496 | bytes 8651264 | tf_op jit(solution)/shard_map/dot_general | solution.py:25
  127.8 4.4 %reshape.87 = bf16[256,2,2048]{2,1,0:T(2,128)(2,1)} reshape(bf16[512,2048]{1,0:T(8,128)(2,1)} %convolution_convert_fusion) | data formatting | bytes 4194304 | tf_op jit(solution)/shard_map/reshape | solution.py:26
  (29 shorter events, 0.6 us)
Async XLA Ops:
  7.2 10.8 %copy-start = (bf16[588,1280]{1,0:T(8,128)(2,1)S(1)}, bf16[588,1280]{1,0:T(8,128)(2,1)}, u32[]{:S(2)}) copy-start(bf16[588,1280]{1,0:T(8,128)(2,1)} %param.15) | copy-start | bytes 4515844
  7.2 1.8 %copy-start.7 = (s32[128,1]{0,1:T(1,128)S(1)}, s32[128,1]{0,1:T(1,128)}, u32[]{:S(2)}) copy-start(s32[128,1]{0,1:T(1,128)} %param.14) | copy-start | bytes 1540
  7.2 104.6 %all-gather.2.cloned.1.call-start = ((), (), s32[]{:S(2)}) async-start(), calls=%async_computation.1 | async-start | bytes 11141120 | tf_op jit(solution)/shard_map/all_gather | solution.py:44
  9.2 8.8 %copy-start.3 = (f32[2,1280]{1,0:T(2,128)S(1)}, f32[2,1280]{1,0:T(2,128)}, u32[]{:S(2)}) copy-start(f32[2,1280]{1,0:T(2,128)} %param.16) | copy-start | bytes 30724
  10.6 31.7 %all-to-all-start = ((bf16[16,16,1177]{2,1,0:T(8,128)(2,1)}), bf16[16,16,1177]{2,1,0:T(8,128)(2,1)S(1)}, u32[]{:S(2)}, u32[]{:S(2)}) async-start(bf16[16,16,1177]{2,1,0:T(8,128)(2,1)} %bitcast.3), calls=%async_computation | async-start | bytes 1310720 | tf_op jit(solution)/shard_map/all_to_all | solution.py:85
  18.0 2.1 %copy-start.5 = (s32[256,1]{0,1:T(1,128)S(1)}, s32[256,1]{0,1:T(1,128)}, u32[]{:S(2)}) copy-start(s32[256,1]{0,1:T(1,128)} %param.11) | copy-start | bytes 3076
  18.0 2.1 %copy-start.4 = (s32[256]{0:T(256)S(1)}, s32[256]{0:T(256)}, u32[]{:S(2)}) copy-start(s32[256]{0:T(256)} %param.12) | copy-start | bytes 3076
  18.0 3.0 %copy-start.1 = (f32[1280]{0:T(1024)S(1)}, f32[1280]{0:T(1024)}, u32[]{:S(2)}) copy-start(f32[1280]{0:T(1024)} %param.18) | copy-start | bytes 15364
  18.1 3.0 %copy-start.2 = (f32[1280]{0:T(1024)S(1)}, f32[1280]{0:T(1024)}, u32[]{:S(2)}) copy-start(f32[1280]{0:T(1024)} %param.17) | copy-start | bytes 15364
  119.2 1.4 copy-start.6
Sparse Core Ops, SparseCore 0:
  10.3 101.4 all-gather.1

commit v2 on v1

--- a/solution.py
+++ b/solution.py
@@ -1,6 +1,10 @@
+import functools
+
 import jax
 import jax.numpy as jnp
 from jax import lax
+from jax.experimental import pallas as pl
+from jax.experimental.pallas import tpu as pltpu
 from jax.sharding import PartitionSpec as P
 
 
@@ -38,12 +42,6 @@
 def slots_of(places, width):
     count = places.shape[0]
     return places[None, :] == lax.broadcasted_iota(jnp.int32, (width, count), 0)
-
-
-def hits_by_gather(cache_rows, hit_owner, hit_slot, pair_weight):
-    gathered = lax.all_gather(cache_rows, "enc", axis=0, tiled=True)
-    rows = jnp.take(gathered, hit_owner * cache_rows.shape[0] + hit_slot, axis=0)
-    return project_pairs(rows, pair_weight)
 
 
 def hits_by_request(cache_rows, hit_owner, hit_slot, pair_weight):
@@ -58,6 +56,343 @@
     answered = lax.all_to_all(stored, "enc", split_axis=0, concat_axis=0, tiled=True)
     answered = answered.reshape((peers * cap,) + answered.shape[2:])
     return project_pairs(jnp.take(answered, places, axis=0), pair_weight)
+
+
+MESH = pl.DeviceIdType.MESH
+HALVES = 2
+
+
+def ring_place(chip, chips):
+    z, y = chip // 2, chip % 2
+    return y * (chips - 1) + z * (1 - 2 * y)
+
+
+def ring_chip(place, chips):
+    y = place // (chips // 2)
+    z = y * (chips - 1) + place * (1 - 2 * y)
+    return 2 * z + y
+
+
+def ring_kernel(
+    peers,
+    pixels,
+    cap,
+    cache_ref,
+    wanted_ref,
+    places_ref,
+    pixel_ref,
+    patch_ref,
+    position_ref,
+    gain_ref,
+    bias_ref,
+    pair_hbm,
+    hit_ref,
+    miss_ref,
+    fresh_ref,
+    held,
+    pair_ref,
+    chosen,
+    encoded,
+    outgoing,
+    incoming,
+    up_send,
+    up_recv,
+    down_send,
+    down_recv,
+    side_send,
+    side_recv,
+    pixel_send,
+    pixel_recv,
+    load_sem,
+    own_sem,
+):
+    chips = peers // 2
+    slots, width = cache_ref.shape
+    half = slots // HALVES
+    embed = width // 2
+    span = pixel_ref.shape[1] // 2
+    pairs = pair_ref.shape[1]
+    steps = chips - 1
+    me = lax.axis_index("enc")
+    chip, core = me // 2, me % 2
+    place = ring_place(chip, chips)
+    above = 2 * ring_chip((place + 1) % chips, chips) + core
+    below = 2 * ring_chip((place + chips - 1) % chips, chips) + core
+    beside = 2 * chip + 1 - core
+
+    barrier = pltpu.get_barrier_semaphore()
+
+    def greet(t, carry):
+        pl.semaphore_signal(
+            barrier, inc=1, device_id={"enc": (me + t) % peers}, device_id_type=MESH
+        )
+        return carry
+
+    lax.fori_loop(1, peers, greet, 0)
+    load = pltpu.make_async_copy(pair_hbm, pair_ref, load_sem)
+    load.start()
+    held[place, pl.ds(core * slots, slots), :] = cache_ref[...]
+    rows = lax.broadcasted_iota(jnp.int32, (peers * cap, places_ref.shape[1]), 0)
+    table = jnp.where(rows == places_ref[...], 1.0, 0.0).astype(jnp.bfloat16)
+    outgoing[...] = jnp.dot(
+        table, pixel_ref[...], preferred_element_type=jnp.float32
+    ).astype(jnp.bfloat16)
+    pl.semaphore_wait(barrier, peers - 1)
+
+    def chunk(owner_place, owner_core, part):
+        return held.at[owner_place, pl.ds(owner_core * slots + part * half, half), :]
+
+    def move(ref, send_sem, recv_sem, target):
+        return pltpu.make_async_remote_copy(
+            src_ref=ref,
+            dst_ref=ref,
+            send_sem=send_sem,
+            recv_sem=recv_sem,
+            device_id={"enc": target},
+            device_id_type=MESH,
+        )
+
+    def up(j, distance):
+        return move(
+            chunk((place + chips - distance) % chips, core, j % 2),
+            up_send.at[j],
+            up_recv.at[j],
+            above,
+        )
+
+    def down(j, distance):
+        return move(
+            chunk((place + distance) % chips, core, 1 - j % 2),
+            down_send.at[j],
+            down_recv.at[j],
+            below,
+        )
+
+    def side(k, whose):
+        if k < 2:
+            ref = chunk(place, whose, k)
+        elif k % 2 == 0:
+            j = (k - 2) // 2
+            ref = chunk((place + chips - j // 2 - 1) % chips, whose, j % 2)
+        else:
+            j = (k - 3) // 2
+            ref = chunk((place + j // 2 + 1) % chips, whose, 1 - j % 2)
+        return move(ref, side_send.at[k], side_recv.at[k], beside)
+
+    sent = []
+
+    def start(copy):
+        copy.start()
+        sent.append(copy)
+
+    for j in range(2):
+        start(up(j, 0))
+        start(down(j, 0))
+    for j in range(2):
+        start(side(j, core))
+
+    def pixel_copy(t, target, source):
+        return pltpu.make_async_remote_copy(
+            src_ref=outgoing.at[pl.ds(target * cap, cap), :],
+            dst_ref=incoming.at[pl.ds(source * cap, cap), :],
+            send_sem=pixel_send.at[t],
+            recv_sem=pixel_recv.at[t],
+            device_id={"enc": target},
+            device_id_type=MESH,
+        )
+
+    def send_pixels(t, carry):
+        pixel_copy(t, (me + t) % peers, me).start()
+        return carry
+
+    lax.fori_loop(1, peers, send_pixels, 0)
+    own = pltpu.make_async_copy(
+        outgoing.at[pl.ds(me * cap, cap), :], incoming.at[pl.ds(me * cap, cap), :], own_sem
+    )
+    own.start()
+
+    def encode(values, patch):
+        embedded = jnp.dot(values, patch_ref[...], preferred_element_type=jnp.float32)
+        embedded = embedded + position_ref[pl.ds(patch, 1), :]
+        return layer_norm(embedded, gain_ref[...], bias_ref[...]).astype(jnp.bfloat16)
+
+    def lanes(index, size):
+        return pl.ds(pl.multiple_of(index * size, size), size)
+
+    def encode_own(patch, carry):
+        encoded[:, lanes(patch, embed)] = encode(pixel_ref[:, lanes(patch, span)], patch)
+        return carry
+
+    tile = 512
+    tiles = pairs // tile
+
+    def project(source, target):
+        def one(i, carry):
+            patch, column = i // tiles, i % tiles
+            target[:, lanes(i, tile)] = jnp.dot(
+                source[:, lanes(patch, embed)],
+                pair_ref[:, lanes(column, tile)],
+                preferred_element_type=jnp.float32,
+            ).astype(jnp.bfloat16)
+            return carry
+
+        lax.fori_loop(0, 2 * tiles, one, 0)
+
+    block = incoming.shape[0] // 2
+
+    def encode_fresh(i, carry):
+        patch, part = i // 2, i % 2
+        here = pl.ds(pl.multiple_of(part * block, block), block)
+        live = incoming[here, pixels : pixels + 1].astype(jnp.float32) > 0
+        fresh = encode(incoming[here, lanes(patch, span)], patch)
+        fresh_ref[here, lanes(patch, embed)] = jnp.where(live, fresh, jnp.zeros_like(fresh))
+        return carry
+
+    def choose(owner_place, first):
+        column = lax.broadcasted_iota(jnp.int32, (wanted_ref.shape[0], 2 * slots), 1)
+        column = column + owner_place * (2 * slots)
+        pick = jnp.where(wanted_ref[...] == column, 1.0, 0.0).astype(jnp.bfloat16)
+
+        def one(i, carry):
+            found = jnp.dot(
+                pick, held[owner_place, :, lanes(i, tile)], preferred_element_type=jnp.float32
+            ).astype(jnp.bfloat16)
+            if first:
+                chosen[:, lanes(i, tile)] = found
+            else:
+                chosen[:, lanes(i, tile)] += found
+            return carry
+
+        lax.fori_loop(0, width // tile, one, 0)
+
+    def wait_side(*copies):
+        for k in copies:
+            side(k, 1 - core).wait_recv()
+
+    lax.fori_loop(0, 2, encode_own, 0)
+    for j in range(steps):
+        up(j, j // 2 + 1).wait_recv()
+        if j + 2 < steps:
+            start(up(j + 2, j // 2 + 1))
+        start(side(2 + 2 * j, core))
+        down(j, j // 2 + 1).wait_recv()
+        if j + 2 < steps:
+            start(down(j + 2, j // 2 + 1))
+        start(side(3 + 2 * j, core))
+        if j == 0:
+            load.wait()
+            project(encoded, miss_ref)
+        elif j == 1:
+            wait_side(0, 1)
+            choose(place, True)
+        elif j == steps - 2:
+
+            def take_pixels(t, carry):
+                pixel_copy(t, me, (me + peers - t) % peers).wait_recv()
+                return carry
+
+            lax.fori_loop(1, peers, take_pixels, 0)
+            own.wait()
+            lax.fori_loop(0, 4, encode_fresh, 0)
+        elif j % 2 == 0:
+            distance = j // 2
+            wait_side(*range(4 * distance - 2, 4 * distance + 2))
+            choose((place + chips - distance) % chips, False)
+            choose((place + distance) % chips, False)
+    wait_side(2 * steps, 2 * steps + 1)
+    choose((place + chips // 2) % chips, False)
+    project(chosen, hit_ref)
+    for copy in sent:
+        copy.wait_send()
+
+    def end_pixels(t, carry):
+        pixel_copy(t, (me + t) % peers, me).wait_send()
+        return carry
+
+    lax.fori_loop(1, peers, end_pixels, 0)
+
+
+def by_ring(
+    cache_rows,
+    hit_owner,
+    hit_slot,
+    miss_pixels,
+    miss_encoder,
+    patch_weight,
+    position,
+    norm_gain,
+    norm_bias,
+    pair_weight,
+):
+    peers = lax.axis_size("enc")
+    slots, patches, embed = cache_rows.shape
+    hits = hit_slot.shape[0]
+    count, _, pixels = miss_pixels.shape
+    pairs = pair_weight.shape[1]
+    cap = 2 * count // peers
+    span = -(-(pixels + 1) // 128) * 128
+    owner = hit_owner[:, 0]
+    place = ring_place(owner // 2, peers // 2) * 2 + owner % 2
+    wanted = (place * slots + hit_slot).reshape(hits, 1)
+    places = fill_places(miss_encoder[:, 0], cap).reshape(1, count)
+    spare = ((0, 0), (0, 0), (0, span - pixels))
+    items = jnp.pad(miss_pixels, spare, constant_values=1).reshape(count, patches * span)
+    patch_rows = jnp.pad(patch_weight, ((0, span - pixels), (0, 0)))
+    bf16 = jnp.bfloat16
+    vmem = pl.BlockSpec(memory_space=pltpu.VMEM)
+    dma = pltpu.SemaphoreType.DMA
+    steps = peers // 2 - 1
+    hit_pairs, miss_pairs, fresh_cache = pl.pallas_call(
+        functools.partial(ring_kernel, peers, pixels, cap),
+        out_shape=(
+            jax.ShapeDtypeStruct((hits, patches * pairs), bf16),
+            jax.ShapeDtypeStruct((count, patches * pairs), bf16),
+            jax.ShapeDtypeStruct((peers * cap, patches * embed), bf16),
+        ),
+        in_specs=[vmem] * 8 + [pl.BlockSpec(memory_space=pl.ANY)],
+        out_specs=(vmem, vmem, vmem),
+        scratch_shapes=[
+            pltpu.VMEM((peers // 2, 2 * slots, patches * embed), bf16),
+            pltpu.VMEM(pair_weight.shape, bf16),
+            pltpu.VMEM((hits, patches * embed), bf16),
+            pltpu.VMEM((count, patches * embed), bf16),
+            pltpu.VMEM((peers * cap, patches * span), bf16),
+            pltpu.VMEM((peers * cap, patches * span), bf16),
+            dma((steps,)),
+            dma((steps,)),
+            dma((steps,)),
+            dma((steps,)),
+            dma((2 * steps + 2,)),
+            dma((2 * steps + 2,)),
+            dma((peers,)),
+            dma((peers,)),
+            dma,
+            dma,
+        ],
+        compiler_params=pltpu.CompilerParams(
+            collective_id=0, has_side_effects=True, vmem_limit_bytes=44 * 1024 * 1024
+        ),
+        cost_estimate=pl.CostEstimate(
+            flops=2 * 2 * (hits + count) * embed * pairs,
+            bytes_accessed=16 * 1024 * 1024,
+            transcendentals=0,
+        ),
+    )(
+        cache_rows.reshape(slots, patches * embed),
+        wanted,
+        places,
+        items,
+        patch_rows,
+        position,
+        norm_gain.reshape(1, embed),
+        norm_bias.reshape(1, embed),
+        pair_weight,
+    )
+    return (
+        hit_pairs.reshape(hits, patches, pairs),
+        miss_pairs.reshape(count, patches, pairs),
+        fresh_cache.reshape(peers * cap, patches, embed),
+    )
 
 
 def local(
@@ -85,8 +420,7 @@
     incoming = lax.all_to_all(outgoing, "enc", split_axis=0, concat_axis=0, tiled=True)
     incoming = incoming.reshape(width, items.shape[1])
     encode = lambda rows: encode_patches(rows, patch_weight, position, norm_gain, norm_bias)
-    hits = hits_by_gather if peers <= 16 else hits_by_request
-    hit_pairs = hits(cache_rows, hit_owner[:, 0], hit_slot, pair_weight)
+    hit_pairs = hits_by_request(cache_rows, hit_owner[:, 0], hit_slot, pair_weight)
     miss_pairs = project_pairs(encode(miss_pixels), pair_weight)
     fresh = encode(incoming[:, : patches * pixels].reshape(width, patches, pixels))
     live = incoming[:, patches * pixels :].reshape(width, 1, 1) > 0
@@ -108,7 +442,7 @@
         P(),
     )
     return jax.shard_map(
-        local,
+        by_ring if mesh.shape["enc"] == 16 else local,
         mesh=mesh,
         in_specs=placed,
         out_specs=(

time: 139 us -> 92.9 us (0.67); the launches traced: 139 us -> 91.5 us
  waiting for transfers between devices: 76.7 us -> 0 us
  Pallas kernels: 0 us -> 76.2 us
  matrix products: 14.8 us -> 0 us
  between operations: 14.3 us -> 0.75 us
  local copies, waits for them, and re-layouts: 22.5 us -> 11.7 us
  starting transfers between devices: 7.42 us -> 0 us
    pallas_call x0 -> x1, Pallas kernels: none -> 76.2 us  [by_ring(): pl.pallas_call(functools.partial(ring_kernel, peers, pixels, cap), out_sh...]
    all_gather x1 -> x0, waiting for transfers between devices: 62.5 us -> none  [hits_by_gather(): gathered = lax.all_gather(cache_rows, 'enc', axis=0, tiled=True)]
    dot_general x5 -> x0, matrix products: 14.8 us -> none  [the longest x2 11.4 us: project_pairs(): jnp.dot(flat_rows, pair_weight, preferred_element_type=jnp.float32)]
    all_to_all x1 -> x0, waiting for transfers between devices: 13.5 us -> none  [local(): lax.all_to_all(outgoing, 'enc', split_axis=0, concat_axis=0, tiled=True)]
    gather x2 -> x0, local copies, waits for them, and re-layouts: 8.76 us -> none  [hits_by_gather(): jnp.take(gathered, hit_owner * cache_rows.shape[0] + hit_slot, axis=0)]
    all_to_all x1 -> x0, starting transfers between devices: 7.38 us -> none  [local(): lax.all_to_all(outgoing, 'enc', split_axis=0, concat_axis=0, tiled=True)]
    select_n x1 -> x0, other arithmetic: 1.98 us -> none  [local(): fresh_cache = jnp.where(live, fresh, jnp.zeros_like(fresh))]
    convert_element_type x2 -> x0, local copies, waits for them, and re-layouts: 1.75 us -> none  [the longest x1 1.08 us: local(): jnp.dot(table, items, preferred_element_type=jnp.float32)]
  transfers between devices with their start and end apart: 2 -> 0, of which waited for: 2 -> 0; matrix products, arithmetic and copies ran while one was open for 15% -> 0% of each run, Pallas kernels for 0% -> 0%
where the time goes in v2:
time: 92.9 us; the launch traced here: 91.5 us
  Pallas kernels  76.2 us (82%)
  local copies, waits for them, and re-layouts  11.7 us (13%)
  other arithmetic  2.8 us (3%)
    pallas_call x1, Pallas kernels, by_ring(): pl.pallas_call(functools.partial(ring_kernel, peers, pixels, cap), out_sh...  76.2 us
    unnamed x13, local copies, waits for them, and re-layouts  3.27 us
    reshape x1, local copies, waits for them, and re-layouts, by_ring(): hit_pairs.reshape(hits, patches, pairs)  2.74 us
    reshape x1, local copies, waits for them, and re-layouts, by_ring(): miss_pairs.reshape(count, patches, pairs)  2.62 us

profile of v2, /device:TPU:0, one launch (start us, length us, event | category | flops | bytes accessed | tf_op | source)
XLA Modules:
  0.0 91.5 jit_solution(5572829477185319244)
XLA Ops:
  0.6 0.0 copy-start.4
  0.6 0.9 select_reduce_fusion
  1.6 1.2 %bitcast_add_fusion.places_ref = s32[1,128]{1,0:T(1,128)} fusion(s32[128]{0:T(128)S(1)} %select_reduce_fusion, s32[128,1]{0,1:T(1,128)} %param.14), kind=kLoop, calls=%fused_computation.16 | loop fusion | flops 256 | bytes 1536 | tf_op jit(solution)/shard_map/add | solution.py:39
  2.7 0.7 multiply_add_fusion
  3.4 0.7 reshape.54.gain_ref
  4.1 0.7 reshape.55.bias_ref
  4.8 0.1 copy.17.wanted_ref
  5.0 0.0 copy-start.3
  5.0 1.6 %copy.18 = bf16[128,2,588]{2,1,0:T(2,128)(2,1)S(1)} copy(bf16[128,2,588]{0,1,2:T(2,128)(2,1)} %param.13) | data formatting | bytes 602112
  6.6 0.3 pad.8.clone
  7.0 0.0 copy-done.4
  7.0 0.1 copy.19
  7.1 0.0 copy-start.1
  7.1 0.0 copy-start.2
  7.1 0.0 copy-done.3
  7.1 0.1 pad.9.patch_ref
  7.2 0.6 copy-done.1
  7.8 0.0 copy-done.2
  7.8 76.2 %shard_map.121 = (bf16[256,4096]{1,0:T(8,128)(2,1)S(1)}, bf16[128,4096]{1,0:T(8,128)(2,1)S(1)}, bf16[256,2560]{1,0:T(8,128)(2,1)S(1)}) custom-call(bf16[128,2560]{1,0:T(8,128)(2,1)S(1)} %bitcast.11, s32[256,1]{1,0:T(8,128)S(1)} %copy.17.wanted_ref, s32[1,128]{1,0:T(1,128)S(1)} %copy-done.2, bf16[128,1280]{1,0:T(8,128)(2,1)S(1)} %bitcast.12, ...), custom_call_target="tpu_custom_call" | custom-call | flops 4026531840 | bytes 16777216 | tf_op jit(solution)/shard_map/pallas_call | solution.py:345
  84.0 0.0 copy-start
  84.0 1.0 %copy-done = bf16[128,4096]{1,0:T(8,128)(2,1)} copy-done((bf16[128,4096]{1,0:T(8,128)(2,1)}, bf16[128,4096]{1,0:T(8,128)(2,1)S(1)}, u32[]{:S(2)}) %copy-start) | copy-done | bytes 1048600
  84.9 2.7 %reshape.56 = bf16[256,2,2048]{2,1,0:T(2,128)(2,1)} reshape(bf16[256,4096]{1,0:T(8,128)(2,1)S(1)} %get-tuple-element.6) | data formatting | bytes 4194304 | tf_op jit(solution)/shard_map/reshape | solution.py:392
  87.7 2.6 %reshape.57 = bf16[128,2,2048]{2,1,0:T(2,128)(2,1)} reshape(bf16[128,4096]{1,0:T(8,128)(2,1)} %copy-done) | data formatting | bytes 2097152 | tf_op jit(solution)/shard_map/reshape | solution.py:393
  90.3 1.2 %reshape.58 = bf16[256,2,1280]{2,1,0:T(2,128)(2,1)} reshape(bf16[256,2560]{1,0:T(8,128)(2,1)S(1)} %get-tuple-element.8) | data formatting | bytes 2621440 | tf_op jit(solution)/shard_map/reshape | solution.py:394
  (1 shorter events, 0.0 us)
Async XLA Ops:
  0.6 6.3 %copy-start.4 = (bf16[128,2,1280]{2,1,0:T(2,128)(2,1)S(1)}, bf16[128,2,1280]{2,1,0:T(2,128)(2,1)}, u32[]{:S(2)}) copy-start(bf16[128,2,1280]{2,1,0:T(2,128)(2,1)} %param.10) | copy-start | bytes 1966084
  5.0 2.1 %copy-start.3 = (bf16[588,1280]{1,0:T(8,128)(2,1)S(1)}, bf16[588,1280]{1,0:T(8,128)(2,1)}, u32[]{:S(2)}) copy-start(bf16[588,1280]{1,0:T(8,128)(2,1)} %param.15) | copy-start | bytes 4515844
  7.1 0.7 copy-start.1
  7.1 0.7 copy-start.2
  84.0 1.0 %copy-start = (bf16[128,4096]{1,0:T(8,128)(2,1)}, bf16[128,4096]{1,0:T(8,128)(2,1)S(1)}, u32[]{:S(2)}) copy-start(bf16[128,4096]{1,0:T(8,128)(2,1)S(1)} %get-tuple-element.7) | copy-start | bytes 3145732

commit v3 on v2

--- a/solution.py
+++ b/solution.py
@@ -78,8 +78,9 @@
     pixels,
     cap,
     cache_ref,
-    wanted_ref,
-    places_ref,
+    owner_ref,
+    slot_ref,
+    encoder_ref,
     pixel_ref,
     patch_ref,
     position_ref,
@@ -132,8 +133,17 @@
     load = pltpu.make_async_copy(pair_hbm, pair_ref, load_sem)
     load.start()
     held[place, pl.ds(core * slots, slots), :] = cache_ref[...]
-    rows = lax.broadcasted_iota(jnp.int32, (peers * cap, places_ref.shape[1]), 0)
-    table = jnp.where(rows == places_ref[...], 1.0, 0.0).astype(jnp.bfloat16)
+    count = encoder_ref.shape[1]
+    named = lax.broadcasted_iota(jnp.int32, (peers, count), 0) == encoder_ref[...]
+    named = jnp.where(named, 1.0, 0.0)
+    item = lax.broadcasted_iota(jnp.int32, (count, count), 0)
+    earlier = item < lax.broadcasted_iota(jnp.int32, (count, count), 1)
+    earlier = jnp.where(earlier, 1.0, 0.0).astype(jnp.bfloat16)
+    before = jnp.dot(named.astype(jnp.bfloat16), earlier, preferred_element_type=jnp.float32)
+    rank = jnp.sum(named * before, axis=0, keepdims=True)
+    places = encoder_ref[...].astype(jnp.float32) * cap + rank
+    rows = lax.broadcasted_iota(jnp.int32, (peers * cap, count), 0).astype(jnp.float32)
+    table = jnp.where(rows == places, 1.0, 0.0).astype(jnp.bfloat16)
     outgoing[...] = jnp.dot(
         table, pixel_ref[...], preferred_element_type=jnp.float32
     ).astype(jnp.bfloat16)
@@ -214,7 +224,7 @@
     def encode(values, patch):
         embedded = jnp.dot(values, patch_ref[...], preferred_element_type=jnp.float32)
         embedded = embedded + position_ref[pl.ds(patch, 1), :]
-        return layer_norm(embedded, gain_ref[...], bias_ref[...]).astype(jnp.bfloat16)
+        return layer_norm(embedded, gain_ref[...][None], bias_ref[...][None]).astype(jnp.bfloat16)
 
     def lanes(index, size):
         return pl.ds(pl.multiple_of(index * size, size), size)
@@ -249,9 +259,10 @@
         return carry
 
     def choose(owner_place, first):
-        column = lax.broadcasted_iota(jnp.int32, (wanted_ref.shape[0], 2 * slots), 1)
-        column = column + owner_place * (2 * slots)
-        pick = jnp.where(wanted_ref[...] == column, 1.0, 0.0).astype(jnp.bfloat16)
+        wanted = owner_ref[...] * slots + slot_ref[...]
+        row = lax.broadcasted_iota(jnp.int32, (2 * slots, wanted.shape[1]), 0)
+        row = row + ring_chip(owner_place, chips) * (2 * slots)
+        pick = jnp.where(wanted == row, 1.0, 0.0).T.astype(jnp.bfloat16)
 
         def one(i, carry):
             found = jnp.dot(
@@ -331,10 +342,6 @@
     pairs = pair_weight.shape[1]
     cap = 2 * count // peers
     span = -(-(pixels + 1) // 128) * 128
-    owner = hit_owner[:, 0]
-    place = ring_place(owner // 2, peers // 2) * 2 + owner % 2
-    wanted = (place * slots + hit_slot).reshape(hits, 1)
-    places = fill_places(miss_encoder[:, 0], cap).reshape(1, count)
     spare = ((0, 0), (0, 0), (0, span - pixels))
     items = jnp.pad(miss_pixels, spare, constant_values=1).reshape(count, patches * span)
     patch_rows = jnp.pad(patch_weight, ((0, span - pixels), (0, 0)))
@@ -349,7 +356,7 @@
             jax.ShapeDtypeStruct((count, patches * pairs), bf16),
             jax.ShapeDtypeStruct((peers * cap, patches * embed), bf16),
         ),
-        in_specs=[vmem] * 8 + [pl.BlockSpec(memory_space=pl.ANY)],
+        in_specs=[vmem] * 9 + [pl.BlockSpec(memory_space=pl.ANY)],
         out_specs=(vmem, vmem, vmem),
         scratch_shapes=[
             pltpu.VMEM((peers // 2, 2 * slots, patches * embed), bf16),
@@ -379,13 +386,14 @@
         ),
     )(
         cache_rows.reshape(slots, patches * embed),
-        wanted,
-        places,
+        hit_owner.reshape(1, hits),
+        hit_slot.reshape(1, hits),
+        miss_encoder.reshape(1, count),
         items,
         patch_rows,
         position,
-        norm_gain.reshape(1, embed),
-        norm_bias.reshape(1, embed),
+        norm_gain,
+        norm_bias,
         pair_weight,
     )
     return (

time: 92.9 us -> 89.8 us (0.967)
  other arithmetic: 2.8 us -> 0 us
    add x2 -> x0, other arithmetic: 1.9 us -> none  [the longest x1 1.18 us: fill_places(): return targets * capacity + rank]
    reshape x3 -> x0, local copies, waits for them, and re-layouts: 1.53 us -> none  [the longest x1 0.7 us: by_ring(): norm_gain.reshape(1, embed)]
    unnamed x13 -> x19, local copies, waits for them, and re-layouts: 3.27 us -> 4.36 us
where the time goes in v3:
time: 89.8 us; the launch traced here: 88.4 us
  Pallas kernels  76.3 us (85%)
  local copies, waits for them, and re-layouts  11.3 us (13%)
    pallas_call x1, Pallas kernels, by_ring(): pl.pallas_call(functools.partial(ring_kernel, peers, pixels, cap), out_sh...  76.3 us
    unnamed x19, local copies, waits for them, and re-layouts  4.36 us
    reshape x1, local copies, waits for them, and re-layouts, by_ring(): hit_pairs.reshape(hits, patches, pairs)  2.74 us
    reshape x1, local copies, waits for them, and re-layouts, by_ring(): miss_pairs.reshape(count, patches, pairs)  2.62 us

profile of v3, /device:TPU:0, one launch (start us, length us, event | category | flops | bytes accessed | tf_op | source)
XLA Modules:
  0.0 88.4 jit_solution(14052572929656042117)
XLA Ops:
  0.6 0.0 copy-start.7
  0.6 1.6 %copy.14 = bf16[128,2,588]{2,1,0:T(2,128)(2,1)S(1)} copy(bf16[128,2,588]{0,1,2:T(2,128)(2,1)} %param.13) | data formatting | bytes 602112
  2.3 0.3 pad.8.clone
  2.6 1.2 %copy.15 = bf16[16,8,2,1280]{3,1,2,0:T(8,128)(2,1)S(1)} copy(bf16[16,8,2,1280]{3,2,1,0:T(2,128)(2,1)} %bitcast.13) | data formatting | bytes 1310720
  3.8 0.0 copy-start.1
  3.8 0.0 copy-start.2
  3.8 0.0 copy-start.3
  3.8 0.0 copy-start.4
  3.8 0.0 copy-start.5
  3.8 0.0 copy-start.6
  3.8 0.0 copy-done.7
  3.8 0.1 pad.9.patch_ref
  4.0 0.5 copy-done.1
  4.5 0.0 copy-done.2
  4.5 0.0 copy-done.3
  4.5 0.0 copy-done.4
  4.5 0.0 copy-done.5
  4.5 0.0 copy-done.6
  4.5 76.3 %shard_map.121 = (bf16[256,4096]{1,0:T(8,128)(2,1)S(1)}, bf16[128,4096]{1,0:T(8,128)(2,1)S(1)}, bf16[256,2560]{1,0:T(8,128)(2,1)S(1)}) custom-call(bf16[128,2560]{1,0:T(8,128)(2,1)S(1)} %bitcast.7, s32[1,256]{1,0:T(1,128)S(1)} %bitcast.9, s32[1,256]{1,0:T(1,128)S(1)} %bitcast.10, s32[1,128]{1,0:T(1,128)S(1)} %bitcast.11, bf16[128,1280]{1,0:T(8,128)(2,1)S(1)} %bitcast.8, ...), custom_call_target="tpu_custom_call" | custom-call | flops 4026531840 | bytes 16777216 | tf_op jit(solution)/shard_map/pallas_call | solution.py:352
  80.9 0.0 copy-start
  80.9 1.0 %copy-done = bf16[128,4096]{1,0:T(8,128)(2,1)} copy-done((bf16[128,4096]{1,0:T(8,128)(2,1)}, bf16[128,4096]{1,0:T(8,128)(2,1)S(1)}, u32[]{:S(2)}) %copy-start) | copy-done | bytes 1048600
  81.8 2.7 %reshape.35 = bf16[256,2,2048]{2,1,0:T(2,128)(2,1)} reshape(bf16[256,4096]{1,0:T(8,128)(2,1)S(1)} %get-tuple-element.6) | data formatting | bytes 4194304 | tf_op jit(solution)/shard_map/reshape | solution.py:400
  84.6 2.6 %reshape.36 = bf16[128,2,2048]{2,1,0:T(2,128)(2,1)} reshape(bf16[128,4096]{1,0:T(8,128)(2,1)} %copy-done) | data formatting | bytes 2097152 | tf_op jit(solution)/shard_map/reshape | solution.py:401
  87.2 1.2 %reshape.37 = bf16[256,2,1280]{2,1,0:T(2,128)(2,1)} reshape(bf16[256,2560]{1,0:T(8,128)(2,1)S(1)} %get-tuple-element.8) | data formatting | bytes 2621440 | tf_op jit(solution)/shard_map/reshape | solution.py:402
  (1 shorter events, 0.0 us)
Async XLA Ops:
  0.6 3.2 %copy-start.7 = (bf16[588,1280]{1,0:T(8,128)(2,1)S(1)}, bf16[588,1280]{1,0:T(8,128)(2,1)}, u32[]{:S(2)}) copy-start(bf16[588,1280]{1,0:T(8,128)(2,1)} %param.15) | copy-start | bytes 4515844
  3.8 0.7 copy-start.1
  3.8 0.7 copy-start.2
  3.8 0.7 copy-start.3
  3.8 0.7 copy-start.4
  3.8 0.7 copy-start.5
  3.8 0.7 copy-start.6
  80.9 1.0 %copy-start = (bf16[128,4096]{1,0:T(8,128)(2,1)}, bf16[128,4096]{1,0:T(8,128)(2,1)S(1)}, u32[]{:S(2)}) copy-start(bf16[128,4096]{1,0:T(8,128)(2,1)S(1)} %get-tuple-element.7) | copy-start | bytes 3145732

commit v4 on v3

--- a/solution.py
+++ b/solution.py
@@ -120,6 +120,13 @@
     above = 2 * ring_chip((place + 1) % chips, chips) + core
     below = 2 * ring_chip((place + chips - 1) % chips, chips) + core
     beside = 2 * chip + 1 - core
+    quarter = place % (chips // 2)
+    cut_up = (quarter % 2) * (1 - quarter // 2)
+    cut_down = (1 - quarter % 2) * (quarter // 2)
+    across = 2 * ring_chip(chips - 1 - place, chips) + core
+    far_up = above + cut_up * (across - above)
+    far_down = below + cut_down * (across - below)
+    far = 4
 
     barrier = pltpu.get_barrier_semaphore()
 
@@ -162,21 +169,34 @@
             device_id_type=MESH,
         )
 
+    def down_part(j):
+        return 1 if j == steps - 1 else j % 2
+
     def up(j, distance):
+        owner = place + chips - distance + (cut_up * (chips // 2) if j >= far else 0)
         return move(
-            chunk((place + chips - distance) % chips, core, j % 2),
+            chunk(owner % chips, core, j % 2),
             up_send.at[j],
             up_recv.at[j],
-            above,
+            far_up if j >= far else above,
         )
 
     def down(j, distance):
+        owner = place + distance + (cut_down * (chips // 2) if j >= far else 0)
         return move(
-            chunk((place + distance) % chips, core, 1 - j % 2),
+            chunk(owner % chips, core, down_part(j)),
             down_send.at[j],
             down_recv.at[j],
-            below,
+            far_down if j >= far else below,
         )
+
+    def up_arrives(j):
+        ref = chunk((place + chips - j // 2 - 1) % chips, core, j % 2)
+        move(ref, up_send.at[j], up_recv.at[j], above).wait_recv()
+
+    def down_arrives(j):
+        ref = chunk((place + j // 2 + 1) % chips, core, down_part(j))
+        move(ref, down_send.at[j], down_recv.at[j], below).wait_recv()
 
     def side(k, whose):
         if k < 2:
@@ -186,7 +206,7 @@
             ref = chunk((place + chips - j // 2 - 1) % chips, whose, j % 2)
         else:
             j = (k - 3) // 2
-            ref = chunk((place + j // 2 + 1) % chips, whose, 1 - j % 2)
+            ref = chunk((place + j // 2 + 1) % chips, whose, down_part(j))
         return move(ref, side_send.at[k], side_recv.at[k], beside)
 
     sent = []
@@ -282,13 +302,17 @@
 
     lax.fori_loop(0, 2, encode_own, 0)
     for j in range(steps):
-        up(j, j // 2 + 1).wait_recv()
-        if j + 2 < steps:
+        up_arrives(j)
+        if j + 2 < far:
             start(up(j + 2, j // 2 + 1))
+        down_arrives(j)
+        if far <= j + 2 < steps:
+            start(up(j + 2, j // 2 + 1))
+        if j + 2 < steps - 1:
+            start(down(j + 2, j // 2 + 1))
+        elif j + 2 == steps:
+            start(down(steps - 1, steps // 2))
         start(side(2 + 2 * j, core))
-        down(j, j // 2 + 1).wait_recv()
-        if j + 2 < steps:
-            start(down(j + 2, j // 2 + 1))
         start(side(3 + 2 * j, core))
         if j == 0:
             load.wait()

time: 89.8 us -> 90.6 us (level); the launches traced: 88.4 us -> 90.3 us
  Pallas kernels: 76.3 us -> 78.3 us
    pallas_call x1, Pallas kernels: 76.3 us -> 78.3 us  [by_ring(): pl.pallas_call(functools.partial(ring_kernel, peers, pixels, cap), out_sh...]
where the time goes in v4:
time: 90.6 us; the launch traced here: 90.3 us
  Pallas kernels  78.3 us (86%)
  local copies, waits for them, and re-layouts  11.3 us (12%)
    pallas_call x1, Pallas kernels, by_ring(): pl.pallas_call(functools.partial(ring_kernel, peers, pixels, cap), out_sh...  78.3 us
    unnamed x19, local copies, waits for them, and re-layouts  4.36 us
    reshape x1, local copies, waits for them, and re-layouts, by_ring(): hit_pairs.reshape(hits, patches, pairs)  2.74 us
    reshape x1, local copies, waits for them, and re-layouts, by_ring(): miss_pairs.reshape(count, patches, pairs)  2.62 us

profile of v4, /device:TPU:0, one launch (start us, length us, event | category | flops | bytes accessed | tf_op | source)
XLA Modules:
  0.0 90.3 jit_solution(13592527992403054528)
XLA Ops:
  0.6 0.0 copy-start.7
  0.6 1.6 %copy.14 = bf16[128,2,588]{2,1,0:T(2,128)(2,1)S(1)} copy(bf16[128,2,588]{0,1,2:T(2,128)(2,1)} %param.13) | data formatting | bytes 602112
  2.3 0.3 pad.8.clone
  2.6 1.2 %copy.15 = bf16[16,8,2,1280]{3,1,2,0:T(8,128)(2,1)S(1)} copy(bf16[16,8,2,1280]{3,2,1,0:T(2,128)(2,1)} %bitcast.13) | data formatting | bytes 1310720
  3.8 0.0 copy-start.1
  3.8 0.0 copy-start.2
  3.8 0.0 copy-start.3
  3.8 0.0 copy-start.4
  3.8 0.0 copy-start.5
  3.8 0.0 copy-start.6
  3.8 0.0 copy-done.7
  3.8 0.1 pad.9.patch_ref
  4.0 0.5 copy-done.1
  4.5 0.0 copy-done.2
  4.5 0.0 copy-done.3
  4.5 0.0 copy-done.4
  4.5 0.0 copy-done.5
  4.5 0.0 copy-done.6
  4.5 78.3 %shard_map.121 = (bf16[256,4096]{1,0:T(8,128)(2,1)S(1)}, bf16[128,4096]{1,0:T(8,128)(2,1)S(1)}, bf16[256,2560]{1,0:T(8,128)(2,1)S(1)}) custom-call(bf16[128,2560]{1,0:T(8,128)(2,1)S(1)} %bitcast.7, s32[1,256]{1,0:T(1,128)S(1)} %bitcast.9, s32[1,256]{1,0:T(1,128)S(1)} %bitcast.10, s32[1,128]{1,0:T(1,128)S(1)} %bitcast.11, bf16[128,1280]{1,0:T(8,128)(2,1)S(1)} %bitcast.8, ...), custom_call_target="tpu_custom_call" | custom-call | flops 4026531840 | bytes 16777216 | tf_op jit(solution)/shard_map/pallas_call | solution.py:376
  82.8 0.0 copy-start
  82.8 1.0 %copy-done = bf16[128,4096]{1,0:T(8,128)(2,1)} copy-done((bf16[128,4096]{1,0:T(8,128)(2,1)}, bf16[128,4096]{1,0:T(8,128)(2,1)S(1)}, u32[]{:S(2)}) %copy-start) | copy-done | bytes 1048600
  83.8 2.7 %reshape.35 = bf16[256,2,2048]{2,1,0:T(2,128)(2,1)} reshape(bf16[256,4096]{1,0:T(8,128)(2,1)S(1)} %get-tuple-element.6) | data formatting | bytes 4194304 | tf_op jit(solution)/shard_map/reshape | solution.py:424
  86.5 2.6 %reshape.36 = bf16[128,2,2048]{2,1,0:T(2,128)(2,1)} reshape(bf16[128,4096]{1,0:T(8,128)(2,1)} %copy-done) | data formatting | bytes 2097152 | tf_op jit(solution)/shard_map/reshape | solution.py:425
  89.1 1.2 %reshape.37 = bf16[256,2,1280]{2,1,0:T(2,128)(2,1)} reshape(bf16[256,2560]{1,0:T(8,128)(2,1)S(1)} %get-tuple-element.8) | data formatting | bytes 2621440 | tf_op jit(solution)/shard_map/reshape | solution.py:426
  (1 shorter events, 0.0 us)
Async XLA Ops:
  0.6 3.2 %copy-start.7 = (bf16[588,1280]{1,0:T(8,128)(2,1)S(1)}, bf16[588,1280]{1,0:T(8,128)(2,1)}, u32[]{:S(2)}) copy-start(bf16[588,1280]{1,0:T(8,128)(2,1)} %param.15) | copy-start | bytes 4515844
  3.8 0.7 copy-start.1
  3.8 0.7 copy-start.2
  3.8 0.7 copy-start.3
  3.8 0.7 copy-start.4
  3.8 0.7 copy-start.5
  3.8 0.7 copy-start.6
  82.8 1.0 %copy-start = (bf16[128,4096]{1,0:T(8,128)(2,1)}, bf16[128,4096]{1,0:T(8,128)(2,1)S(1)}, u32[]{:S(2)}) copy-start(bf16[128,4096]{1,0:T(8,128)(2,1)S(1)} %get-tuple-element.7) | copy-start | bytes 3145732

commit v5 on v4

--- a/solution.py
+++ b/solution.py
@@ -235,7 +235,6 @@
         pixel_copy(t, (me + t) % peers, me).start()
         return carry
 
-    lax.fori_loop(1, peers, send_pixels, 0)
     own = pltpu.make_async_copy(
         outgoing.at[pl.ds(me * cap, cap), :], incoming.at[pl.ds(me * cap, cap), :], own_sem
     )
@@ -314,6 +313,8 @@
             start(down(steps - 1, steps // 2))
         start(side(2 + 2 * j, core))
         start(side(3 + 2 * j, core))
+        if j == 3:
+            lax.fori_loop(1, peers, send_pixels, 0)
         if j == 0:
             load.wait()
             project(encoded, miss_ref)

time: 90.6 us -> 88.6 us (0.978)
  Pallas kernels: 78.3 us -> 76.3 us
    pallas_call x1, Pallas kernels: 78.3 us -> 76.3 us  [by_ring(): pl.pallas_call(functools.partial(ring_kernel, peers, pixels, cap), out_sh...]
where the time goes in v5:
time: 88.6 us; the launch traced here: 88.4 us
  Pallas kernels  76.3 us (86%)
  local copies, waits for them, and re-layouts  11.3 us (13%)
    pallas_call x1, Pallas kernels, by_ring(): pl.pallas_call(functools.partial(ring_kernel, peers, pixels, cap), out_sh...  76.3 us
    unnamed x19, local copies, waits for them, and re-layouts  4.36 us
    reshape x1, local copies, waits for them, and re-layouts, by_ring(): hit_pairs.reshape(hits, patches, pairs)  2.74 us
    reshape x1, local copies, waits for them, and re-layouts, by_ring(): miss_pairs.reshape(count, patches, pairs)  2.62 us

profile of v5, /device:TPU:0, one launch (start us, length us, event | category | flops | bytes accessed | tf_op | source)
XLA Modules:
  0.0 88.4 jit_solution(3478486088252858098)
XLA Ops:
  0.6 0.0 copy-start.7
  0.6 1.6 %copy.14 = bf16[128,2,588]{2,1,0:T(2,128)(2,1)S(1)} copy(bf16[128,2,588]{0,1,2:T(2,128)(2,1)} %param.13) | data formatting | bytes 602112
  2.3 0.3 pad.8.clone
  2.6 1.2 %copy.15 = bf16[16,8,2,1280]{3,1,2,0:T(8,128)(2,1)S(1)} copy(bf16[16,8,2,1280]{3,2,1,0:T(2,128)(2,1)} %bitcast.13) | data formatting | bytes 1310720
  3.8 0.0 copy-start.1
  3.8 0.0 copy-start.2
  3.8 0.0 copy-start.3
  3.8 0.0 copy-start.4
  3.8 0.0 copy-start.5
  3.8 0.0 copy-start.6
  3.8 0.0 copy-done.7
  3.8 0.1 pad.9.patch_ref
  4.0 0.5 copy-done.1
  4.5 0.0 copy-done.2
  4.5 0.0 copy-done.3
  4.5 0.0 copy-done.4
  4.5 0.0 copy-done.5
  4.5 0.0 copy-done.6
  4.5 76.3 %shard_map.121 = (bf16[256,4096]{1,0:T(8,128)(2,1)S(1)}, bf16[128,4096]{1,0:T(8,128)(2,1)S(1)}, bf16[256,2560]{1,0:T(8,128)(2,1)S(1)}) custom-call(bf16[128,2560]{1,0:T(8,128)(2,1)S(1)} %bitcast.7, s32[1,256]{1,0:T(1,128)S(1)} %bitcast.9, s32[1,256]{1,0:T(1,128)S(1)} %bitcast.10, s32[1,128]{1,0:T(1,128)S(1)} %bitcast.11, bf16[128,1280]{1,0:T(8,128)(2,1)S(1)} %bitcast.8, ...), custom_call_target="tpu_custom_call" | custom-call | flops 4026531840 | bytes 16777216 | tf_op jit(solution)/shard_map/pallas_call | solution.py:377
  80.9 0.0 copy-start
  80.9 1.0 %copy-done = bf16[128,4096]{1,0:T(8,128)(2,1)} copy-done((bf16[128,4096]{1,0:T(8,128)(2,1)}, bf16[128,4096]{1,0:T(8,128)(2,1)S(1)}, u32[]{:S(2)}) %copy-start) | copy-done | bytes 1048600
  81.8 2.7 %reshape.35 = bf16[256,2,2048]{2,1,0:T(2,128)(2,1)} reshape(bf16[256,4096]{1,0:T(8,128)(2,1)S(1)} %get-tuple-element.6) | data formatting | bytes 4194304 | tf_op jit(solution)/shard_map/reshape | solution.py:425
  84.6 2.6 %reshape.36 = bf16[128,2,2048]{2,1,0:T(2,128)(2,1)} reshape(bf16[128,4096]{1,0:T(8,128)(2,1)} %copy-done) | data formatting | bytes 2097152 | tf_op jit(solution)/shard_map/reshape | solution.py:426
  87.2 1.2 %reshape.37 = bf16[256,2,1280]{2,1,0:T(2,128)(2,1)} reshape(bf16[256,2560]{1,0:T(8,128)(2,1)S(1)} %get-tuple-element.8) | data formatting | bytes 2621440 | tf_op jit(solution)/shard_map/reshape | solution.py:427
  (1 shorter events, 0.0 us)
Async XLA Ops:
  0.6 3.2 %copy-start.7 = (bf16[588,1280]{1,0:T(8,128)(2,1)S(1)}, bf16[588,1280]{1,0:T(8,128)(2,1)}, u32[]{:S(2)}) copy-start(bf16[588,1280]{1,0:T(8,128)(2,1)} %param.15) | copy-start | bytes 4515844
  3.8 0.7 copy-start.1
  3.8 0.7 copy-start.2
  3.8 0.7 copy-start.3
  3.8 0.7 copy-start.4
  3.8 0.7 copy-start.5
  3.8 0.7 copy-start.6
  80.9 1.0 %copy-start = (bf16[128,4096]{1,0:T(8,128)(2,1)}, bf16[128,4096]{1,0:T(8,128)(2,1)S(1)}, u32[]{:S(2)}) copy-start(bf16[128,4096]{1,0:T(8,128)(2,1)S(1)} %get-tuple-element.7) | copy-start | bytes 3145732

commit v6 on v5

--- a/solution.py
+++ b/solution.py
@@ -321,20 +321,19 @@
         elif j == 1:
             wait_side(0, 1)
             choose(place, True)
-        elif j == steps - 2:
-
-            def take_pixels(t, carry):
-                pixel_copy(t, me, (me + peers - t) % peers).wait_recv()
-                return carry
-
-            lax.fori_loop(1, peers, take_pixels, 0)
-            own.wait()
-            lax.fori_loop(0, 4, encode_fresh, 0)
         elif j % 2 == 0:
             distance = j // 2
             wait_side(*range(4 * distance - 2, 4 * distance + 2))
             choose((place + chips - distance) % chips, False)
             choose((place + distance) % chips, False)
+
+    def take_pixels(t, carry):
+        pixel_copy(t, me, (me + peers - t) % peers).wait_recv()
+        return carry
+
+    lax.fori_loop(1, peers, take_pixels, 0)
+    own.wait()
+    lax.fori_loop(0, 4, encode_fresh, 0)
     wait_side(2 * steps, 2 * steps + 1)
     choose((place + chips // 2) % chips, False)
     project(chosen, hit_ref)

time: 88.6 us -> 91.7 us (1.035)
  Pallas kernels: 76.3 us -> 79.4 us
    pallas_call x1, Pallas kernels: 76.3 us -> 79.4 us  [by_ring(): pl.pallas_call(functools.partial(ring_kernel, peers, pixels, cap), out_sh...]
where the time goes in v6:
time: 91.7 us; the launch traced here: 91.5 us
  Pallas kernels  79.4 us (87%)
  local copies, waits for them, and re-layouts  11.3 us (12%)
    pallas_call x1, Pallas kernels, by_ring(): pl.pallas_call(functools.partial(ring_kernel, peers, pixels, cap), out_sh...  79.4 us
    unnamed x19, local copies, waits for them, and re-layouts  4.36 us
    reshape x1, local copies, waits for them, and re-layouts, by_ring(): hit_pairs.reshape(hits, patches, pairs)  2.74 us
    reshape x1, local copies, waits for them, and re-layouts, by_ring(): miss_pairs.reshape(count, patches, pairs)  2.62 us

profile of v6, /device:TPU:0, one launch (start us, length us, event | category | flops | bytes accessed | tf_op | source)
XLA Modules:
  0.0 91.5 jit_solution(5574481878126590840)
XLA Ops:
  0.6 0.0 copy-start.7
  0.6 1.6 %copy.14 = bf16[128,2,588]{2,1,0:T(2,128)(2,1)S(1)} copy(bf16[128,2,588]{0,1,2:T(2,128)(2,1)} %param.13) | data formatting | bytes 602112
  2.3 0.3 pad.8.clone
  2.6 1.2 %copy.15 = bf16[16,8,2,1280]{3,1,2,0:T(8,128)(2,1)S(1)} copy(bf16[16,8,2,1280]{3,2,1,0:T(2,128)(2,1)} %bitcast.13) | data formatting | bytes 1310720
  3.8 0.0 copy-start.1
  3.8 0.0 copy-start.2
  3.8 0.0 copy-start.3
  3.8 0.0 copy-start.4
  3.8 0.0 copy-start.5
  3.8 0.0 copy-start.6
  3.8 0.0 copy-done.7
  3.8 0.1 pad.9.patch_ref
  4.0 0.5 copy-done.1
  4.5 0.0 copy-done.2
  4.5 0.0 copy-done.3
  4.5 0.0 copy-done.4
  4.5 0.0 copy-done.5
  4.5 0.0 copy-done.6
  4.5 79.4 %shard_map.121 = (bf16[256,4096]{1,0:T(8,128)(2,1)S(1)}, bf16[128,4096]{1,0:T(8,128)(2,1)S(1)}, bf16[256,2560]{1,0:T(8,128)(2,1)S(1)}) custom-call(bf16[128,2560]{1,0:T(8,128)(2,1)S(1)} %bitcast.7, s32[1,256]{1,0:T(1,128)S(1)} %bitcast.9, s32[1,256]{1,0:T(1,128)S(1)} %bitcast.10, s32[1,128]{1,0:T(1,128)S(1)} %bitcast.11, bf16[128,1280]{1,0:T(8,128)(2,1)S(1)} %bitcast.8, ...), custom_call_target="tpu_custom_call" | custom-call | flops 4026531840 | bytes 16777216 | tf_op jit(solution)/shard_map/pallas_call | solution.py:376
  83.9 0.0 copy-start
  83.9 1.0 %copy-done = bf16[128,4096]{1,0:T(8,128)(2,1)} copy-done((bf16[128,4096]{1,0:T(8,128)(2,1)}, bf16[128,4096]{1,0:T(8,128)(2,1)S(1)}, u32[]{:S(2)}) %copy-start) | copy-done | bytes 1048600
  84.9 2.7 %reshape.35 = bf16[256,2,2048]{2,1,0:T(2,128)(2,1)} reshape(bf16[256,4096]{1,0:T(8,128)(2,1)S(1)} %get-tuple-element.6) | data formatting | bytes 4194304 | tf_op jit(solution)/shard_map/reshape | solution.py:424
  87.6 2.6 %reshape.36 = bf16[128,2,2048]{2,1,0:T(2,128)(2,1)} reshape(bf16[128,4096]{1,0:T(8,128)(2,1)} %copy-done) | data formatting | bytes 2097152 | tf_op jit(solution)/shard_map/reshape | solution.py:425
  90.2 1.2 %reshape.37 = bf16[256,2,1280]{2,1,0:T(2,128)(2,1)} reshape(bf16[256,2560]{1,0:T(8,128)(2,1)S(1)} %get-tuple-element.8) | data formatting | bytes 2621440 | tf_op jit(solution)/shard_map/reshape | solution.py:426
  (1 shorter events, 0.0 us)
Async XLA Ops:
  0.6 3.2 %copy-start.7 = (bf16[588,1280]{1,0:T(8,128)(2,1)S(1)}, bf16[588,1280]{1,0:T(8,128)(2,1)}, u32[]{:S(2)}) copy-start(bf16[588,1280]{1,0:T(8,128)(2,1)} %param.15) | copy-start | bytes 4515844
  3.8 0.7 copy-start.1
  3.8 0.7 copy-start.2
  3.8 0.7 copy-start.3
  3.8 0.7 copy-start.4
  3.8 0.7 copy-start.5
  3.8 0.7 copy-start.6
  83.9 1.0 %copy-start = (bf16[128,4096]{1,0:T(8,128)(2,1)}, bf16[128,4096]{1,0:T(8,128)(2,1)S(1)}, u32[]{:S(2)}) copy-start(bf16[128,4096]{1,0:T(8,128)(2,1)S(1)} %get-tuple-element.7) | copy-start | bytes 3145732
